TPU v7x, 32 devices: a whole 2x2x4 slice. The times are simulated.
32 devices in a mesh: groups: 2 (over y), ctx: 4 (over z), chan: 4 (over x, core).
Axes of the slice: x: 2, y: 2, z: 4, core: 2. Of those that a mesh axis runs over, the one named last changes fastest.
Arguments:
- projected: bfloat16 [3, 2048, 4096], P(None, ('groups', 'ctx'), 'chan'), parts along dimension 1, may hold values from -6 to 6
- short_filter: float32 [3, 3, 4096], P(None, None, 'chan'), may hold values from -3 to 3
- decay_rates: float32 [16, 4096], P(None, 'chan'), may hold values from 0.0001953125 to 0.05
- residues: float32 [16, 4096], P(None, 'chan'), may hold values from -1.5 to 1.5
- skip_gain: float32 [4096], P('chan'), may hold values from -4 to 4
- out_weight: bfloat16 [4096, 2048], P('chan'), may hold values from -0.09375 to 0.09375
Outputs:
- layer_out: bfloat16 [2048, 2048], P(('groups', 'ctx'), 'chan'), parts along dimension 0
There are 2 independent parts, one for each index of `groups`. A program takes and returns all parts, laid end to end along the dimension named above; an argument that names none is the same for every part. Nothing has to cross between parts.
All inputs are finite; a program needn't handle non-finite values.
Results may differ from a plain program's by a relative error of at most 0.012.
Values may be sent and summed in bfloat16 or wider, within the bound.
A program may use at most 128 MiB of HBM per device.

v0:
```python
import functools

import jax
import jax.numpy as jnp
from jax import lax
from jax.experimental import pallas as pl
from jax.experimental.pallas import tpu as pltpu
from jax.sharding import PartitionSpec as P

MESH = pl.DeviceIdType.MESH
LANES = 128
SUB = 8
STEP = 16


def parts_of(length):
    return [(0, length // 4), (length // 4, length // 4), (length // 2, length // 2)]


def expm1(v):
    series = jnp.ones_like(v)
    for order in range(9, 1, -1):
        series = 1.0 + series * v * (1.0 / order)
    return jnp.where(v > -0.3, v * series, jnp.exp(v) - 1.0)


def rows(token, count=1):
    start = token * SUB
    if not isinstance(start, int):
        start = pl.multiple_of(start, SUB)
    return pl.ds(start, count * SUB)


def kernel(
    n, m, proj_hbm, sf_hbm, dr_hbm, re_hbm, sg_hbm, w_hbm, out_ref,
    proj, sf_ref, dr_ref, re_ref, sg_ref, wv, sft, dec, res, skip, decay, gain, passing, first_pow,
    sixth, eighth, lead, stored, x, q, g, y, mo, own, arrived, carried, ss, sr, xs, xr, acc,
    proj_sem, small_sem, w_sem, edge_send, edge_recv, state_send, state_recv,
    sib_send, sib_recv, far_send, far_recv,
):
    length, width = proj.shape[1:]
    modes = dr_ref.shape[0]
    blocks = width // LANES
    half = m // 2
    out_w = out_ref.shape[1]
    parts = parts_of(length)
    z, c = lax.axis_index("ctx"), lax.axis_index("chan")
    hi, lo = c // 2, lax.rem(c, 2)
    sibling = hi * 2 + (1 - lo)

    def far(o):
        return lax.rem(hi + o, half) * 2 + lo

    barrier = pltpu.get_barrier_semaphore()
    for off in range(1, n):
        pl.semaphore_signal(barrier, inc=1, device_id={"ctx": lax.rem(z + off, n)}, device_id_type=MESH)
    pl.semaphore_signal(barrier, inc=1, device_id={"chan": sibling}, device_id_type=MESH)
    for o in range(1, half):
        pl.semaphore_signal(barrier, inc=1, device_id={"chan": far(o)}, device_id_type=MESH)

    quarter = length // 4

    def proj_copy(comp, piece):
        token = pl.ds(piece * quarter, quarter)
        return pltpu.make_async_copy(
            proj_hbm.at[comp, token, :], proj.at[comp, token, :], proj_sem.at[comp, piece]
        )

    small = [
        pltpu.make_async_copy(source, target, small_sem.at[index])
        for index, (source, target) in enumerate(
            ((dr_hbm, dr_ref), (re_hbm, re_ref), (sf_hbm, sf_ref), (sg_hbm, sg_ref))
        )
    ]
    for piece in range(4):
        for comp in (1, 2):
            proj_copy(comp, piece).start()
        small[piece].start()
    for piece in range(4):
        proj_copy(0, piece).start()

    def w_copy(o, who):
        target = lax.rem(hi + o, half) * 2 + (lo if who else 1 - lo)
        columns = pl.ds(pl.multiple_of(target * out_w, LANES), out_w)
        slot = 2 * o + who
        return pltpu.make_async_copy(w_hbm.at[:, columns], wv.at[slot], w_sem.at[slot])

    if blocks < SUB:
        for buffer in (sft, dec, res, skip, x):
            buffer[...] = jnp.zeros_like(buffer)

    span = blocks * STEP

    def permutation(height, depth, source):
        row = lax.broadcasted_iota(jnp.int32, (height, depth), 0)
        column = lax.broadcasted_iota(jnp.int32, (height, depth), 1)
        return jnp.where(source(row) == column, 1.0, 0.0).astype(jnp.bfloat16)

    to_token = permutation(STEP * SUB, span, lambda row: (row % SUB) * STEP + row // SUB)
    to_block = permutation(span, STEP * SUB, lambda row: (row % STEP) * SUB + row // STEP)

    def relay(comps, piece):
        for comp in comps:
            proj_copy(comp, piece).wait()
        for t in range(piece * quarter, (piece + 1) * quarter, STEP):
            stacked = [
                jnp.concatenate(
                    [proj[comp, pl.ds(t, STEP), pl.ds(j * LANES, LANES)] for j in range(blocks)], axis=0
                )
                for comp in comps
            ]
            moved = jnp.dot(
                to_token, jnp.concatenate(stacked, axis=1), preferred_element_type=jnp.float32
            )
            for index, comp in enumerate(comps):
                x[comp, rows(t + 2, STEP), :] = moved[:, index * LANES : (index + 1) * LANES]

    for piece in range(4):
        relay((1, 2), piece)

    def edge(index, comp, count):
        return pltpu.make_async_remote_copy(
            src_ref=x.at[pl.ds(comp, count), pl.ds(length * SUB, 2 * SUB), :],
            dst_ref=x.at[pl.ds(comp, count), pl.ds(0, 2 * SUB), :],
            send_sem=edge_send.at[index],
            recv_sem=edge_recv.at[index],
            device_id={"ctx": lax.rem(z + 1, n)},
            device_id_type=MESH,
        )

    pl.semaphore_wait(barrier, (n - 1) + 1 + (half - 1))

    @pl.when(z < n - 1)
    def _():
        edge(0, 1, 2).start()

    for o in list(range(1, half)) + [0]:
        for who in range(2):
            w_copy(o, who).start()

    for copy in small:
        copy.wait()
    for j in range(blocks):
        lanes = pl.ds(j * LANES, LANES)
        dec[pl.ds(j, modes, stride=SUB), :] = dr_ref[:, lanes]
        res[pl.ds(j, modes, stride=SUB), :] = re_ref[:, lanes]
        skip[pl.ds(j, 1), :] = sg_ref[:, lanes]
        for comp in range(3):
            sft[pl.ds(comp * 3 * SUB + j, 3, stride=SUB), :] = sf_ref[comp, :, lanes]
    rate = dec[...]
    decay[...] = jnp.exp(-rate)
    first_pow[...] = jnp.exp(-rate * float(length - 2))
    sixth[...] = jnp.exp(-rate * float(SUB - 2))
    eighth[...] = jnp.exp(-rate * float(SUB))

    def mode(ref, k):
        return ref[pl.ds(k * SUB, SUB), :]

    def short(comp, t, count):
        total = None
        for lag in range(3):
            value = x[comp, rows(t + 2 - lag, count), :].reshape(count, SUB, LANES)
            value = mode(sft, comp * 3 + lag)[None] * value
            total = value if total is None else total + value
        return total

    def mix(t, count):
        gated = (short(1, t, count) * short(2, t, count)).astype(jnp.bfloat16).astype(jnp.float32)
        g[rows(t, count), :] = gated.reshape(count * SUB, LANES)
        return gated

    once = [mode(decay, k) for k in range(modes)]
    twice = [value * value for value in once]

    def horner(state, gated, count):
        for s in range(0, count, 2):
            state = [
                twice[k] * state[k] + (once[k] * gated[s] + gated[s + 1]) for k in range(modes)
            ]
        return state

    state = horner([jnp.zeros((SUB, LANES), jnp.float32)] * modes, mix(2, SUB - 2), SUB - 2)

    def held(i, k):
        return pl.ds(pl.multiple_of((i * modes + k) * SUB, SUB), SUB)

    def own_lap(i, state):
        for k in range(modes):
            stored[held(i, k), :] = state[k]
        return tuple(horner(list(state), mix(i * SUB, SUB), SUB))

    state = list(lax.fori_loop(1, length // SUB, own_lap, tuple(state)))

    @pl.when(z == 0)
    def _():
        x[:, pl.ds(0, 2 * SUB), :] = jnp.zeros((3, 2 * SUB, LANES), jnp.float32)

    @pl.when(z > 0)
    def _():
        edge(0, 1, 2).wait_recv()

    head = mix(0, 2)
    for k in range(0, modes, 2):
        pair = [state[k + e] + mode(first_pow, k + e) * (once[k + e] * head[0] + head[1]) for e in range(2)]
        own[pl.ds(k * SUB, 2 * SUB), :] = jnp.concatenate(pair, axis=0).astype(jnp.bfloat16)

    def send_state(off):
        return pltpu.make_async_remote_copy(
            src_ref=own,
            dst_ref=arrived.at[off - 1],
            send_sem=state_send.at[off - 1],
            recv_sem=state_recv.at[off - 1],
            device_id={"ctx": lax.rem(z + off, n)},
            device_id_type=MESH,
        )

    for off in range(1, n):

        @pl.when(z + off < n)
        def _(off=off):
            send_state(off).start()

    for piece in range(4):
        relay((0,), piece)

    @pl.when(z < n - 1)
    def _():
        edge(1, 0, 1).start()

    gain[...] = res[...] * jnp.sqrt(-expm1(-2.0 * rate))
    passing[...] = jnp.exp(-rate * float(length))
    lead[...] = gain[...] * decay[...]
    power = [mode(gain, k) for k in range(modes)]
    taps = []
    for lag in range(SUB):
        total = skip[...] if lag == 0 else jnp.zeros((SUB, LANES), jnp.float32)
        for k in range(modes):
            total = total + power[k]
            power[k] = power[k] * once[k]
        taps.append(total)

    @pl.loop(0, length // SUB)
    def _(i):
        gated = [g[rows(i * SUB + s), :] for s in range(SUB)]
        for s in range(SUB):
            total = taps[0] * gated[s]
            for lag in range(1, s + 1):
                total = total + taps[lag] * gated[s - lag]
            y[rows(i * SUB + s), :] = total

    @pl.when(z > 0)
    def _():
        edge(1, 0, 1).wait_recv()

    @pl.loop(0, length // STEP)
    def _(i):
        t = i * STEP
        q[rows(t, STEP), :] = short(0, t, STEP).reshape(STEP * SUB, LANES)

    carried[...] = jnp.zeros_like(carried)
    for off in range(n - 1, 0, -1):

        @pl.when(z >= off)
        def _(off=off):
            send_state(off).wait_recv()
            carried[...] = carried[...] * passing[...] + arrived[off - 1].astype(jnp.float32)

    def finish(i, start_state):
        reach = [mode(lead, k) * start_state[k] for k in range(modes)]
        for s in range(SUB):
            token = rows(i * SUB + s)
            sums = [y[token, :], None, None, None]
            for k in range(modes):
                sums[k % 4] = reach[k] if sums[k % 4] is None else sums[k % 4] + reach[k]
                if s < SUB - 1:
                    reach[k] = reach[k] * once[k]
            y[token, :] = q[token, :] * ((sums[0] + sums[1]) + (sums[2] + sums[3]))

    def finish_lap(i, past):
        finish(i, [stored[held(i, k), :] + past[k] for k in range(modes)])
        return tuple(past[k] * mode(eighth, k) for k in range(modes))

    finish(0, [mode(carried, k) for k in range(modes)])
    past = [
        mode(sixth, k) * (twice[k] * mode(carried, k) + (once[k] * head[0] + head[1])) for k in range(modes)
    ]

    def gather(start):
        groups = [
            y[rows(start + e * STEP, STEP), :].astype(jnp.bfloat16) for e in range(quarter // STEP)
        ]
        moved = jnp.dot(
            to_block, jnp.concatenate(groups, axis=1), preferred_element_type=jnp.float32
        ).astype(jnp.bfloat16)
        for e in range(quarter // STEP):
            for j in range(blocks):
                mo[pl.ds(start + e * STEP, STEP), pl.ds(j * LANES, LANES)] = moved[
                    j * STEP : (j + 1) * STEP, e * LANES : (e + 1) * LANES
                ]

    def to_sibling(o, p):
        token = pl.ds(*parts[p]) if o else pl.ds(0, length)
        return pltpu.make_async_remote_copy(
            src_ref=ss.at[o, token, :],
            dst_ref=sr.at[o, token, :],
            send_sem=sib_send.at[o, p],
            recv_sem=sib_recv.at[o, p],
            device_id={"chan": sibling},
            device_id_type=MESH,
        )

    def to_far(o, p):
        token = pl.ds(*parts[p])
        return pltpu.make_async_remote_copy(
            src_ref=xs.at[o - 1, token, :],
            dst_ref=xr.at[o - 1, token, :],
            send_sem=far_send.at[o - 1, p],
            recv_sem=far_recv.at[o - 1, p],
            device_id={"chan": far(o)},
            device_id_type=MESH,
        )

    def product(token, slot):
        return jnp.dot(mo[token, :], wv[slot], preferred_element_type=jnp.float32)

    def forward(p):
        token = pl.ds(*parts[p])
        for o in range(1, half):
            to_sibling(o, p).wait_recv()
            xs[o - 1, token, :] = (acc[o, token, :] + sr[o, token, :].astype(jnp.float32)).astype(jnp.bfloat16)
            to_far(o, p).start()

    for p, (start, count) in enumerate(parts):
        token = pl.ds(start, count)
        past = lax.fori_loop(max(1, start // SUB), (start + count) // SUB, finish_lap, tuple(past))
        for first in range(start, start + count, quarter):
            gather(first)
        if p > 0:
            forward(p - 1)
        for o in range(1, half):
            if p == 0:
                w_copy(o, 0).wait()
            ss[o, token, :] = product(token, 2 * o).astype(jnp.bfloat16)
            to_sibling(o, p).start()
        for o in range(1, half):
            if p == 0:
                w_copy(o, 1).wait()
            acc[o, token, :] = product(token, 2 * o + 1)

    every = pl.ds(0, length)
    w_copy(0, 0).wait()
    ss[0] = product(every, 0).astype(jnp.bfloat16)
    to_sibling(0, 0).start()
    forward(len(parts) - 1)
    w_copy(0, 1).wait()
    acc[0] = product(every, 1)
    to_sibling(0, 0).wait_recv()
    for p, (start, count) in enumerate(parts):
        token = pl.ds(start, count)
        total = acc[0, token, :] + sr[0, token, :].astype(jnp.float32)
        for o in range(1, half):
            to_far(o, p).wait_recv()
            total = total + xr[o - 1, token, :].astype(jnp.float32)
        out_ref[token, :] = total.astype(out_ref.dtype)

    @pl.when(z < n - 1)
    def _():
        edge(0, 1, 2).wait_send()
        edge(1, 0, 1).wait_send()

    for off in range(1, n):

        @pl.when(z + off < n)
        def _(off=off):
            send_state(off).wait_send()

    to_sibling(0, 0).wait_send()
    for p in range(len(parts)):
        for o in range(1, half):
            to_sibling(o, p).wait_send()
            to_far(o, p).wait_send()


def body(projected, short_filter, decay_rates, residues, skip_gain, out_weight):
    n, m = lax.axis_size("ctx"), lax.axis_size("chan")
    length, width = projected.shape[1:]
    modes = decay_rates.shape[0]
    out_w = out_weight.shape[1] // m
    half = m // 2
    count = len(parts_of(length))
    f32, bf16 = jnp.float32, jnp.bfloat16
    table = pltpu.VMEM((modes * SUB, LANES), f32)
    tokens = pltpu.VMEM((length * SUB, LANES), f32)
    dma = pltpu.SemaphoreType.DMA
    vmem = pl.BlockSpec(memory_space=pltpu.VMEM)
    hbm = pl.BlockSpec(memory_space=pltpu.HBM)
    return pl.pallas_call(
        functools.partial(kernel, n, m),
        out_shape=pltpu.VMEM((length, out_w), bf16),
        in_specs=[hbm] * 6,
        out_specs=vmem,
        scratch_shapes=[
            pltpu.VMEM((3, length, width), bf16),
            pltpu.VMEM(short_filter.shape, f32),
            pltpu.VMEM(decay_rates.shape, f32),
            pltpu.VMEM(residues.shape, f32),
            pltpu.VMEM((1, width), f32),
            pltpu.VMEM((m, width, out_w), bf16),
            pltpu.VMEM((9 * SUB, LANES), f32),
            table,
            table,
            pltpu.VMEM((SUB, LANES), f32),
            table,
            table,
            table,
            table,
            table,
            table,
            table,
            pltpu.VMEM((length // SUB * modes * SUB, LANES), f32),
            pltpu.VMEM((3, (length + 2) * SUB, LANES), f32),
            tokens,
            tokens,
            tokens,
            pltpu.VMEM((length, width), bf16),
            pltpu.VMEM((modes * SUB, LANES), bf16),
            pltpu.VMEM((n - 1, modes * SUB, LANES), bf16),
            table,
            pltpu.VMEM((half, length, out_w), bf16),
            pltpu.VMEM((half, length, out_w), bf16),
            pltpu.VMEM((half - 1, length, out_w), bf16),
            pltpu.VMEM((half - 1, length, out_w), bf16),
            pltpu.VMEM((half, length, out_w), f32),
            dma((3, 4)),
            dma((4,)),
            dma((m,)),
            dma((2,)),
            dma((2,)),
            dma((n - 1,)),
            dma((n - 1,)),
            dma((half, count)),
            dma((half, count)),
            dma((half - 1, count)),
            dma((half - 1, count)),
        ],
        compiler_params=pltpu.CompilerParams(
            collective_id=0, has_side_effects=True, vmem_limit_bytes=60 * 1024 * 1024
        ),
        cost_estimate=pl.CostEstimate(
            flops=2 * length * width * out_w * m, bytes_accessed=2 * width * out_w * m, transcendentals=0
        ),
        name="hyena_layer",
    )(projected, short_filter, decay_rates, residues, skip_gain.reshape(1, width), out_weight)


def solution(mesh):
    in_specs = (
        P(None, ("groups", "ctx"), "chan"),
        P(None, None, "chan"),
        P(None, "chan"),
        P(None, "chan"),
        P("chan"),
        P("chan", None),
    )
    out_specs = P(("groups", "ctx"), "chan")
    return jax.shard_map(body, mesh=mesh, in_specs=in_specs, out_specs=out_specs, check_vma=False)
```

profile of v0, /device:TPU:16, one launch (start us, length us, event | category | flops | bytes accessed | tf_op | source)
XLA Modules:
  0.0 21.0 jit_solution(8907979923914360866)
XLA Ops:
  0.0 20.3 %hyena_layer.1 = bf16[256,512]{1,0:T(8,128)(2,1)S(1)} custom-call(bf16[3,256,1024]{2,1,0:T(8,128)(2,1)} %proj_hbm.1, f32[3,3,1024]{2,1,0:T(4,128)} %sf_hbm.1, f32[16,1024]{1,0:T(8,128)} %dr_hbm.1, f32[16,1024]{1,0:T(8,128)} %re_hbm.1, f32[1,1024]{1,0:T(1,128)} %bitcast.1, bf16[1024,2048]{1,0:T(8,128)(2,1)} %w_hbm.1), custom_call_target="tpu_custom_call" | custom-call | flops 1073741824 | bytes 4194304 | tf_op jit(solution)/shard_map/hyena_layer/pallas_call | solution.py:397
  20.3 0.7 %copy.8 = bf16[256,512]{1,0:T(8,128)(2,1)} copy(bf16[256,512]{1,0:T(8,128)(2,1)S(1)} %hyena_layer.1) | data formatting | bytes 524288
where the time goes:
time: 21.1 us; the launch traced here: 21 us
  Pallas kernels  20.3 us (96%)
  local copies, waits for them, and re-layouts  0.71 us (3%)
    pallas_call x1, Pallas kernels, body(): pl.pallas_call(functools.partial(kernel, n, m), out_shape=pltpu.VMEM((len...  20.3 us
    unnamed x1, local copies, waits for them, and re-layouts  0.71 us

commit v1 on v0

--- a/solution.py
+++ b/solution.py
@@ -72,10 +72,10 @@
             ((dr_hbm, dr_ref), (re_hbm, re_ref), (sf_hbm, sf_ref), (sg_hbm, sg_ref))
         )
     ]
-    for piece in range(4):
+    for index, piece in enumerate((3, 0, 1, 2)):
         for comp in (1, 2):
             proj_copy(comp, piece).start()
-        small[piece].start()
+        small[index].start()
     for piece in range(4):
         proj_copy(0, piece).start()
 
@@ -115,8 +115,7 @@
             for index, comp in enumerate(comps):
                 x[comp, rows(t + 2, STEP), :] = moved[:, index * LANES : (index + 1) * LANES]
 
-    for piece in range(4):
-        relay((1, 2), piece)
+    relay((1, 2), 3)
 
     def edge(index, comp, count):
         return pltpu.make_async_remote_copy(
@@ -133,6 +132,9 @@
     @pl.when(z < n - 1)
     def _():
         edge(0, 1, 2).start()
+
+    for piece in range(3):
+        relay((1, 2), piece)
 
     for o in list(range(1, half)) + [0]:
         for who in range(2):
@@ -172,24 +174,30 @@
     once = [mode(decay, k) for k in range(modes)]
     twice = [value * value for value in once]
 
-    def horner(state, gated, count):
+    def horner(group, state, gated, count):
         for s in range(0, count, 2):
             state = [
-                twice[k] * state[k] + (once[k] * gated[s] + gated[s + 1]) for k in range(modes)
+                twice[k] * value + (once[k] * gated[s] + gated[s + 1]) for k, value in zip(group, state)
             ]
         return state
 
-    state = horner([jnp.zeros((SUB, LANES), jnp.float32)] * modes, mix(2, SUB - 2), SUB - 2)
-
     def held(i, k):
         return pl.ds(pl.multiple_of((i * modes + k) * SUB, SUB), SUB)
 
-    def own_lap(i, state):
-        for k in range(modes):
-            stored[held(i, k), :] = state[k]
-        return tuple(horner(list(state), mix(i * SUB, SUB), SUB))
-
-    state = list(lax.fori_loop(1, length // SUB, own_lap, tuple(state)))
+    zero = jnp.zeros((SUB, LANES), jnp.float32)
+    groups = [range(0, modes // 2), range(modes // 2, modes)]
+
+    def own_lap(group, gated_of, i, state):
+        for k, value in zip(group, state):
+            stored[held(i, k), :] = value
+        return tuple(horner(group, list(state), gated_of(i * SUB, SUB), SUB))
+
+    def own_pass(group, gated_of):
+        state = horner(group, [zero] * len(group), gated_of(2, SUB - 2), SUB - 2)
+        lap = functools.partial(own_lap, group, gated_of)
+        return lax.fori_loop(1, length // SUB, lap, tuple(state))
+
+    state = own_pass(groups[0], mix)
 
     @pl.when(z == 0)
     def _():
@@ -200,25 +208,37 @@
         edge(0, 1, 2).wait_recv()
 
     head = mix(0, 2)
-    for k in range(0, modes, 2):
-        pair = [state[k + e] + mode(first_pow, k + e) * (once[k + e] * head[0] + head[1]) for e in range(2)]
-        own[pl.ds(k * SUB, 2 * SUB), :] = jnp.concatenate(pair, axis=0).astype(jnp.bfloat16)
-
-    def send_state(off):
+
+    def send_state(off, part):
+        piece = pl.ds(groups[part][0] * SUB, len(groups[part]) * SUB)
         return pltpu.make_async_remote_copy(
-            src_ref=own,
-            dst_ref=arrived.at[off - 1],
-            send_sem=state_send.at[off - 1],
-            recv_sem=state_recv.at[off - 1],
+            src_ref=own.at[piece, :],
+            dst_ref=arrived.at[off - 1, piece, :],
+            send_sem=state_send.at[off - 1, part],
+            recv_sem=state_recv.at[off - 1, part],
             device_id={"ctx": lax.rem(z + off, n)},
             device_id_type=MESH,
         )
 
-    for off in range(1, n):
-
-        @pl.when(z + off < n)
-        def _(off=off):
-            send_state(off).start()
+    def publish(part, state):
+        group = groups[part]
+        whole = [
+            value + mode(first_pow, k) * (once[k] * head[0] + head[1]) for k, value in zip(group, state)
+        ]
+        for index in range(0, len(group), 2):
+            pair = jnp.concatenate(whole[index : index + 2], axis=0)
+            own[pl.ds(group[index] * SUB, 2 * SUB), :] = pair.astype(jnp.bfloat16)
+        for off in range(1, n):
+
+            @pl.when(z + off < n)
+            def _(off=off):
+                send_state(off, part).start()
+
+    def mixed_before(t, count):
+        return g[rows(t, count), :].reshape(count, SUB, LANES)
+
+    publish(0, state)
+    publish(1, own_pass(groups[1], mixed_before))
 
     for piece in range(4):
         relay((0,), piece)
@@ -262,7 +282,8 @@
 
         @pl.when(z >= off)
         def _(off=off):
-            send_state(off).wait_recv()
+            for part in range(2):
+                send_state(off, part).wait_recv()
             carried[...] = carried[...] * passing[...] + arrived[off - 1].astype(jnp.float32)
 
     def finish(i, start_state):
@@ -286,11 +307,11 @@
     ]
 
     def gather(start):
-        groups = [
+        columns = [
             y[rows(start + e * STEP, STEP), :].astype(jnp.bfloat16) for e in range(quarter // STEP)
         ]
         moved = jnp.dot(
-            to_block, jnp.concatenate(groups, axis=1), preferred_element_type=jnp.float32
+            to_block, jnp.concatenate(columns, axis=1), preferred_element_type=jnp.float32
         ).astype(jnp.bfloat16)
         for e in range(quarter // STEP):
             for j in range(blocks):
@@ -372,7 +393,8 @@
 
         @pl.when(z + off < n)
         def _(off=off):
-            send_state(off).wait_send()
+            for part in range(2):
+                send_state(off, part).wait_send()
 
     to_sibling(0, 0).wait_send()
     for p in range(len(parts)):
@@ -436,8 +458,8 @@
             dma((m,)),
             dma((2,)),
             dma((2,)),
-            dma((n - 1,)),
-            dma((n - 1,)),
+            dma((n - 1, 2)),
+            dma((n - 1, 2)),
             dma((half, count)),
             dma((half, count)),
             dma((half - 1, count)),

time: 21.1 us -> 21.3 us (level)
  the two profiles are of different devices: /device:TPU:16 before, /device:TPU:0 now
where the time goes in v1:
time: 21.3 us; the launch traced here: 20.9 us
  Pallas kernels  20.2 us (95%)
  local copies, waits for them, and re-layouts  0.71 us (3%)
    pallas_call x1, Pallas kernels, body(): pl.pallas_call(functools.partial(kernel, n, m), out_shape=pltpu.VMEM((len...  20.2 us
    unnamed x1, local copies, waits for them, and re-layouts  0.71 us

profile of v1, /device:TPU:0, one launch (start us, length us, event | category | flops | bytes accessed | tf_op | source)
XLA Modules:
  0.0 20.9 jit_solution(7181518158008808820)
XLA Ops:
  0.0 20.2 %hyena_layer.1 = bf16[256,512]{1,0:T(8,128)(2,1)S(1)} custom-call(bf16[3,256,1024]{2,1,0:T(8,128)(2,1)} %proj_hbm.1, f32[3,3,1024]{2,1,0:T(4,128)} %sf_hbm.1, f32[16,1024]{1,0:T(8,128)} %dr_hbm.1, f32[16,1024]{1,0:T(8,128)} %re_hbm.1, f32[1,1024]{1,0:T(1,128)} %bitcast.1, bf16[1024,2048]{1,0:T(8,128)(2,1)} %w_hbm.1), custom_call_target="tpu_custom_call" | custom-call | flops 1073741824 | bytes 4194304 | tf_op jit(solution)/shard_map/hyena_layer/pallas_call | solution.py:419
  20.2 0.7 %copy.8 = bf16[256,512]{1,0:T(8,128)(2,1)} copy(bf16[256,512]{1,0:T(8,128)(2,1)S(1)} %hyena_layer.1) | data formatting | bytes 524288
